TPU v7x, 512 devices: a whole 4x8x8 slice. The times are simulated.
512 devices in a mesh: dp: 8 (over y_lo, core), ctx: 64 (over z, y_hi, x).
Axes of the slice: x: 4, y: 8 (y_hi: 2, y_lo: 4; y = y_hi * 4 + y_lo), z: 8, core: 2. Of those that a mesh axis runs over, the one named last changes fastest.
Arguments:
- query_rows: bfloat16 [512, 256, 2048], P(('dp', 'ctx')), parts along dimension 0, may hold values from -32 to 32
- key_rows: bfloat16 [512, 256, 2048], P(('dp', 'ctx')), parts along dimension 0, may hold values from -32 to 32
- value_rows: bfloat16 [512, 256, 2048], P(('dp', 'ctx')), parts along dimension 0, may hold values from -6 to 6
Outputs:
- temporal_out: bfloat16 [512, 256, 2048], P(('dp', 'ctx')), parts along dimension 0
There are 8 independent parts, one for each index of `dp`. A program takes and returns all parts, laid end to end along the dimension named above; each array names one. Nothing has to cross between parts.
All inputs are finite; a program needn't handle non-finite values.
Results may differ from a plain program's by a relative error of at most 0.0064.
Values may be sent and summed in bfloat16 or wider, within the bound.
A program may use at most 64 MiB of HBM per device.

v0:
```python
import functools
import math

import jax
import jax.numpy as jnp
from jax import lax
from jax.experimental import pallas as pl
from jax.experimental.pallas import tpu as pltpu
from jax.sharding import PartitionSpec as P

HEADS = 16
HD = 128
TOK = 256
FRAMES = 64
WIDTH = HEADS * HD
SLOTS = 4
CHUNKS = HEADS // SLOTS
PLACES = 16
MESH = pl.DeviceIdType.MESH
SCALE = HD**-0.5 * math.log2(math.e)
STRIDE = 27


def attend(q, k, v, keep=None):
    scores = lax.dot_general(q, k, (((1,), (1,)), ((), ())), preferred_element_type=jnp.float32)
    if keep is not None:
        scores = jnp.where(keep, scores, -jnp.inf)
    top = jnp.max(scores, axis=1, keepdims=True)
    weights = jnp.exp2((scores - top) * SCALE)
    total = jnp.sum(weights, axis=1, keepdims=True)
    weights = (weights * (1.0 / total)).astype(jnp.bfloat16)
    return jnp.dot(weights, v, preferred_element_type=jnp.float32)


def kernel(q_hbm, k_hbm, v_hbm, o_hbm, qk, v, mid, r_qk, r_v, turned, back, o_part, out, load, s_qk, s_v, s_o, g_qk, g_v, g_o, store):
    clip, me = lax.axis_index("dp"), lax.axis_index("ctx")
    loads = [
        pltpu.make_async_copy(q_hbm, qk.at[0], load.at[0]),
        pltpu.make_async_copy(k_hbm, qk.at[1], load.at[1]),
        pltpu.make_async_copy(v_hbm, v, load.at[2]),
    ]
    for copy in loads:
        copy.start()

    def at(peer):
        return {"dp": clip, "ctx": peer}

    def peer_of(i):
        r = lax.rem(i * STRIDE, FRAMES)
        x = lax.rem(lax.rem(me, 4) + lax.rem(r, 4), 4)
        y = lax.rem(lax.rem(me // 4, 2) + lax.rem(r // 4, 2), 2)
        z = lax.rem(me // 8 + r // 8, 8)
        return (z * 2 + y) * 4 + x

    barrier = pltpu.get_barrier_semaphore()

    @pl.loop(1, FRAMES)
    def _(i):
        pl.semaphore_signal(barrier, inc=1, device_id=at(peer_of(i)), device_id_type=MESH)

    pl.semaphore_wait(barrier, FRAMES - 1)

    def block(chunk, peer):
        rows = pl.ds(pl.multiple_of((peer // SLOTS) * PLACES, PLACES), PLACES)
        cols = pl.ds(pl.multiple_of((chunk * SLOTS + lax.rem(peer, SLOTS)) * HD, HD), HD)
        return rows, cols

    def send_qk(chunk):
        rows, cols = block(chunk, me)
        pltpu.make_async_copy(qk.at[:, rows, cols], r_qk.at[chunk, :, me], g_qk.at[chunk]).start()

        @pl.loop(1, FRAMES)
        def _(i):
            peer = peer_of(i)
            rows, cols = block(chunk, peer)
            pltpu.make_async_remote_copy(
                src_ref=qk.at[:, rows, cols], dst_ref=r_qk.at[chunk, :, me],
                send_sem=s_qk.at[chunk], recv_sem=g_qk.at[chunk],
                device_id=at(peer), device_id_type=MESH,
            ).start()

    def send_mid(chunk):
        rows, cols = block(chunk, me)
        pltpu.make_async_copy(mid.at[rows, cols], r_v.at[chunk, me], g_v.at[chunk]).start()

        @pl.loop(1, FRAMES)
        def _(i):
            peer = peer_of(i)
            rows, cols = block(chunk, peer)
            pltpu.make_async_remote_copy(
                src_ref=mid.at[rows, cols], dst_ref=r_v.at[chunk, me],
                send_sem=s_v.at[chunk], recv_sem=g_v.at[chunk],
                device_id=at(peer), device_id_type=MESH,
            ).start()

    def send_back(chunk):
        rows, cols = block(chunk, me)
        pltpu.make_async_copy(o_part.at[chunk, me], out.at[rows, cols], g_o.at[chunk]).start()

        @pl.loop(1, FRAMES)
        def _(i):
            peer = peer_of(i)
            pltpu.make_async_remote_copy(
                src_ref=o_part.at[chunk, peer], dst_ref=out.at[rows, cols],
                send_sem=s_o.at[chunk], recv_sem=g_o.at[chunk],
                device_id=at(peer), device_id_type=MESH,
            ).start()

    def arrived(ref, sem):
        pltpu.make_async_copy(ref, ref, sem).wait()

    def spatial(chunk):
        @pl.loop(0, SLOTS)
        def _(slot):
            cols = pl.ds(pl.multiple_of((chunk * SLOTS + slot) * HD, HD), HD)
            mid[:, cols] = attend(qk[0, :, cols], qk[1, :, cols], v[:, cols]).astype(jnp.bfloat16)

    side = lax.broadcasted_iota(jnp.int32, (2 * FRAMES, 2 * FRAMES), 0) // FRAMES
    other = lax.broadcasted_iota(jnp.int32, (2 * FRAMES, 2 * FRAMES), 1) // FRAMES
    keep = side == other

    def temporal(chunk):
        turned[0] = r_qk[chunk, 0].reshape(FRAMES * PLACES, HD).astype(jnp.float32)
        turned[1] = r_qk[chunk, 1].reshape(FRAMES * PLACES, HD).astype(jnp.float32)
        turned[2] = r_v[chunk].reshape(FRAMES * PLACES, HD).astype(jnp.float32)
        for t in range(0, PLACES, 2):
            trio = [
                jnp.concatenate(
                    [turned[a, pl.ds(t + s, FRAMES, stride=PLACES), :] for s in range(2)], axis=0
                ).astype(jnp.bfloat16)
                for a in range(3)
            ]
            both = attend(*trio, keep)
            back[pl.ds(t, FRAMES, stride=PLACES), :] = both[:FRAMES]
            back[pl.ds(t + 1, FRAMES, stride=PLACES), :] = both[FRAMES:]
        o_part[chunk] = back[...].astype(jnp.bfloat16).reshape(FRAMES, PLACES, HD)

    loads[0].wait()
    loads[1].wait()

    @pl.loop(0, CHUNKS)
    def _(chunk):
        send_qk(chunk)

    loads[2].wait()

    @pl.loop(0, CHUNKS)
    def _(chunk):
        spatial(chunk)
        send_mid(chunk)

    @pl.loop(0, CHUNKS)
    def _(chunk):
        arrived(r_qk.at[chunk], g_qk.at[chunk])
        arrived(r_v.at[chunk], g_v.at[chunk])
        temporal(chunk)
        send_back(chunk)

    def result(chunk):
        cols = pl.ds(pl.multiple_of(chunk * SLOTS * HD, SLOTS * HD), SLOTS * HD)
        return pltpu.make_async_copy(out.at[:, cols], o_hbm.at[:, cols], store.at[chunk])

    for chunk in range(CHUNKS):
        cols = pl.ds(chunk * SLOTS * HD, SLOTS * HD)
        arrived(out.at[:, cols], g_o.at[chunk])
        result(chunk).start()
    for chunk in range(CHUNKS):
        sent = pl.ds(0, FRAMES - 1)
        arrived(r_qk.at[chunk, :, sent], s_qk.at[chunk])
        arrived(r_v.at[chunk, sent], s_v.at[chunk])
        arrived(o_part.at[chunk, sent], s_o.at[chunk])
        result(chunk).wait()


def local(query_rows, key_rows, value_rows):
    shape = query_rows.shape
    rows = (TOK, WIDTH)
    anywhere = pl.BlockSpec(memory_space=pl.ANY)
    sem = pltpu.SemaphoreType.DMA
    result = pl.pallas_call(
        kernel,
        out_shape=jax.ShapeDtypeStruct(rows, jnp.bfloat16),
        in_specs=[anywhere] * 3,
        out_specs=anywhere,
        scratch_shapes=[
            pltpu.VMEM((2,) + rows, jnp.bfloat16),
            pltpu.VMEM(rows, jnp.bfloat16),
            pltpu.VMEM(rows, jnp.bfloat16),
            pltpu.VMEM((CHUNKS, 2, FRAMES, PLACES, HD), jnp.bfloat16),
            pltpu.VMEM((CHUNKS, FRAMES, PLACES, HD), jnp.bfloat16),
            pltpu.VMEM((3, FRAMES * PLACES, HD), jnp.float32),
            pltpu.VMEM((FRAMES * PLACES, HD), jnp.float32),
            pltpu.VMEM((CHUNKS, FRAMES, PLACES, HD), jnp.bfloat16),
            pltpu.VMEM(rows, jnp.bfloat16),
            sem((3,)),
        ]
        + [sem((CHUNKS,))] * 7,
        compiler_params=pltpu.CompilerParams(
            collective_id=0, has_side_effects=True, vmem_limit_bytes=48 * 1024 * 1024
        ),
        name="two_cores",
    )(query_rows.reshape(rows), key_rows.reshape(rows), value_rows.reshape(rows))
    return result.reshape(shape)


def solution(mesh):
    spec = P(("dp", "ctx"), None, None)
    return jax.shard_map(local, mesh=mesh, in_specs=(spec,) * 3, out_specs=spec, check_vma=False)
```

profile of v0, /device:TPU:1, one launch (start us, length us, event | category | flops | bytes accessed | tf_op | source)
XLA Modules:
  0.0 121.3 jit_solution(12393673029867643159)
XLA Ops:
  0.0 0.0 copy-start
  0.0 1.2 %copy-done = bf16[1,256,2048]{2,1,0:T(8,128)(2,1)S(1)} copy-done((bf16[1,256,2048]{2,1,0:T(8,128)(2,1)S(1)}, bf16[1,256,2048]{2,1,0:T(8,128)(2,1)}, u32[]{:S(2)}) %copy-start) | copy-done | bytes 1048600
  1.2 0.0 copy-start.1
  1.2 1.2 %copy-done.1 = bf16[1,256,2048]{2,1,0:T(8,128)(2,1)S(1)} copy-done((bf16[1,256,2048]{2,1,0:T(8,128)(2,1)S(1)}, bf16[1,256,2048]{2,1,0:T(8,128)(2,1)}, u32[]{:S(2)}) %copy-start.1) | copy-done | bytes 1048600
  2.5 0.0 copy-start.2
  2.5 1.2 %copy-done.2 = bf16[1,256,2048]{2,1,0:T(8,128)(2,1)S(1)} copy-done((bf16[1,256,2048]{2,1,0:T(8,128)(2,1)S(1)}, bf16[1,256,2048]{2,1,0:T(8,128)(2,1)}, u32[]{:S(2)}) %copy-start.2) | copy-done | bytes 1048600
  3.7 116.7 %two_cores.1 = bf16[256,2048]{1,0:T(8,128)(2,1)S(1)} custom-call(bf16[256,2048]{1,0:T(8,128)(2,1)S(1)} %bitcast.5, bf16[256,2048]{1,0:T(8,128)(2,1)S(1)} %bitcast.6, bf16[256,2048]{1,0:T(8,128)(2,1)S(1)} %bitcast.7), custom_call_target="tpu_custom_call" | custom-call | tf_op jit(solution)/shard_map/two_cores/pallas_call | solution.py:180
  120.4 1.0 copy.5
Async XLA Ops:
  0.0 1.2 %copy-start = (bf16[1,256,2048]{2,1,0:T(8,128)(2,1)S(1)}, bf16[1,256,2048]{2,1,0:T(8,128)(2,1)}, u32[]{:S(2)}) copy-start(bf16[1,256,2048]{2,1,0:T(8,128)(2,1)} %param.3) | copy-start | bytes 3145732
  1.2 1.2 %copy-start.1 = (bf16[1,256,2048]{2,1,0:T(8,128)(2,1)S(1)}, bf16[1,256,2048]{2,1,0:T(8,128)(2,1)}, u32[]{:S(2)}) copy-start(bf16[1,256,2048]{2,1,0:T(8,128)(2,1)} %param.4) | copy-start | bytes 3145732
  2.5 1.2 %copy-start.2 = (bf16[1,256,2048]{2,1,0:T(8,128)(2,1)S(1)}, bf16[1,256,2048]{2,1,0:T(8,128)(2,1)}, u32[]{:S(2)}) copy-start(bf16[1,256,2048]{2,1,0:T(8,128)(2,1)} %param.5) | copy-start | bytes 3145732
where the time goes:
time: 122 us; the launch traced here: 121 us
  Pallas kernels  117 us (96%)
  local copies, waits for them, and re-layouts  4.65 us (4%)
    pallas_call x1, Pallas kernels, local(): pl.pallas_call(kernel, out_shape=jax.ShapeDtypeStruct(rows, jnp.bfloat16)...  117 us
    unnamed x7, local copies, waits for them, and re-layouts  4.65 us

commit v1 on v0

--- a/solution.py
+++ b/solution.py
@@ -18,7 +18,14 @@
 PLACES = 16
 MESH = pl.DeviceIdType.MESH
 SCALE = HD**-0.5 * math.log2(math.e)
-STRIDE = 27
+LINE = 8
+FLAT = 8
+STRIDE = 37
+REST_STRIDE = 18
+FAR_FIRST = sorted(
+    range(1, FRAMES),
+    key=lambda r: -(min(r // 8, 8 - r // 8) + 4 * (r // 4 % 2) + 0.5 * min(r % 4, 4 - r % 4)),
+)
 
 
 def attend(q, k, v, keep=None):
@@ -32,7 +39,7 @@
     return jnp.dot(weights, v, preferred_element_type=jnp.float32)
 
 
-def kernel(q_hbm, k_hbm, v_hbm, o_hbm, qk, v, mid, r_qk, r_v, turned, back, o_part, out, load, s_qk, s_v, s_o, g_qk, g_v, g_o, store):
+def kernel(q_hbm, k_hbm, v_hbm, o_hbm, qk, v, mid, r_qk, r_v, turned, back, o_part, ready, load, s_qk, s_v, s_o, g_qk, g_v, g_o):
     clip, me = lax.axis_index("dp"), lax.axis_index("ctx")
     loads = [
         pltpu.make_async_copy(q_hbm, qk.at[0], load.at[0]),
@@ -45,39 +52,55 @@
     def at(peer):
         return {"dp": clip, "ctx": peer}
 
-    def peer_of(i):
+    x, y, z = lax.rem(me, 4), lax.rem(me // 4, 2), me // 8
+
+    def moved(flat, line):
+        new_x, new_y = lax.rem(x + lax.rem(flat, 4), 4), lax.rem(y + flat // 4, 2)
+        return (lax.rem(z + line, LINE) * 2 + new_y) * 4 + new_x
+
+    def every(i):
         r = lax.rem(i * STRIDE, FRAMES)
-        x = lax.rem(lax.rem(me, 4) + lax.rem(r, 4), 4)
-        y = lax.rem(lax.rem(me // 4, 2) + lax.rem(r // 4, 2), 2)
-        z = lax.rem(me // 8 + r // 8, 8)
-        return (z * 2 + y) * 4 + x
+        return moved(lax.rem(r, FLAT), r // FLAT)
+
+    def rest(i):
+        r = lax.rem(i * REST_STRIDE, (FLAT - 1) * (LINE - 1))
+        return moved(r // (LINE - 1) + 1, lax.rem(r, LINE - 1) + 1)
 
     barrier = pltpu.get_barrier_semaphore()
-
-    @pl.loop(1, FRAMES)
-    def _(i):
-        pl.semaphore_signal(barrier, inc=1, device_id=at(peer_of(i)), device_id_type=MESH)
-
-    pl.semaphore_wait(barrier, FRAMES - 1)
+    for i in range(1, LINE):
+        pl.semaphore_signal(barrier, inc=1, device_id=at(moved(0, i)), device_id_type=MESH)
+    for i in range(1, FLAT):
+        pl.semaphore_signal(barrier, inc=1, device_id=at(moved(i, 0)), device_id_type=MESH)
+    pl.semaphore_wait(barrier, LINE + FLAT - 2)
+    for i in range(1, FLAT):
+        pl.semaphore_signal(ready, inc=1, device_id=at(moved(i, 0)), device_id_type=MESH)
 
     def block(chunk, peer):
         rows = pl.ds(pl.multiple_of((peer // SLOTS) * PLACES, PLACES), PLACES)
         cols = pl.ds(pl.multiple_of((chunk * SLOTS + lax.rem(peer, SLOTS)) * HD, HD), HD)
         return rows, cols
 
-    def send_qk(chunk):
+    def send_qk(chunk, peer):
+        rows, cols = block(chunk, peer)
+        pltpu.make_async_remote_copy(
+            src_ref=qk.at[:, rows, cols], dst_ref=r_qk.at[chunk, :, me],
+            send_sem=s_qk.at[chunk], recv_sem=g_qk.at[chunk],
+            device_id=at(peer), device_id_type=MESH,
+        ).start()
+
+    def send_qk_near(chunk):
         rows, cols = block(chunk, me)
         pltpu.make_async_copy(qk.at[:, rows, cols], r_qk.at[chunk, :, me], g_qk.at[chunk]).start()
 
-        @pl.loop(1, FRAMES)
+        @pl.loop(1, LINE)
         def _(i):
-            peer = peer_of(i)
-            rows, cols = block(chunk, peer)
-            pltpu.make_async_remote_copy(
-                src_ref=qk.at[:, rows, cols], dst_ref=r_qk.at[chunk, :, me],
-                send_sem=s_qk.at[chunk], recv_sem=g_qk.at[chunk],
-                device_id=at(peer), device_id_type=MESH,
-            ).start()
+            send_qk(chunk, moved(i, 0))
+            send_qk(chunk, moved(0, i))
+
+    def send_qk_rest(chunk):
+        @pl.loop(0, (FLAT - 1) * (LINE - 1))
+        def _(i):
+            send_qk(chunk, rest(i))
 
     def send_mid(chunk):
         rows, cols = block(chunk, me)
@@ -85,7 +108,7 @@
 
         @pl.loop(1, FRAMES)
         def _(i):
-            peer = peer_of(i)
+            peer = every(i)
             rows, cols = block(chunk, peer)
             pltpu.make_async_remote_copy(
                 src_ref=mid.at[rows, cols], dst_ref=r_v.at[chunk, me],
@@ -95,13 +118,12 @@
 
     def send_back(chunk):
         rows, cols = block(chunk, me)
-        pltpu.make_async_copy(o_part.at[chunk, me], out.at[rows, cols], g_o.at[chunk]).start()
-
-        @pl.loop(1, FRAMES)
-        def _(i):
-            peer = peer_of(i)
+        pltpu.make_async_copy(o_part.at[chunk, me], o_hbm.at[rows, cols], g_o.at[chunk]).start()
+
+        for r in FAR_FIRST:
+            peer = moved(r % FLAT, r // FLAT)
             pltpu.make_async_remote_copy(
-                src_ref=o_part.at[chunk, peer], dst_ref=out.at[rows, cols],
+                src_ref=o_part.at[chunk, peer], dst_ref=o_hbm.at[rows, cols],
                 send_sem=s_o.at[chunk], recv_sem=g_o.at[chunk],
                 device_id=at(peer), device_id_type=MESH,
             ).start()
@@ -140,7 +162,13 @@
 
     @pl.loop(0, CHUNKS)
     def _(chunk):
-        send_qk(chunk)
+        send_qk_near(chunk)
+
+    pl.semaphore_wait(ready, FLAT - 1)
+
+    @pl.loop(0, CHUNKS)
+    def _(chunk):
+        send_qk_rest(chunk)
 
     loads[2].wait()
 
@@ -156,20 +184,14 @@
         temporal(chunk)
         send_back(chunk)
 
-    def result(chunk):
-        cols = pl.ds(pl.multiple_of(chunk * SLOTS * HD, SLOTS * HD), SLOTS * HD)
-        return pltpu.make_async_copy(out.at[:, cols], o_hbm.at[:, cols], store.at[chunk])
-
     for chunk in range(CHUNKS):
         cols = pl.ds(chunk * SLOTS * HD, SLOTS * HD)
-        arrived(out.at[:, cols], g_o.at[chunk])
-        result(chunk).start()
+        arrived(o_hbm.at[:, cols], g_o.at[chunk])
     for chunk in range(CHUNKS):
         sent = pl.ds(0, FRAMES - 1)
         arrived(r_qk.at[chunk, :, sent], s_qk.at[chunk])
         arrived(r_v.at[chunk, sent], s_v.at[chunk])
         arrived(o_part.at[chunk, sent], s_o.at[chunk])
-        result(chunk).wait()
 
 
 def local(query_rows, key_rows, value_rows):
@@ -191,12 +213,12 @@
             pltpu.VMEM((3, FRAMES * PLACES, HD), jnp.float32),
             pltpu.VMEM((FRAMES * PLACES, HD), jnp.float32),
             pltpu.VMEM((CHUNKS, FRAMES, PLACES, HD), jnp.bfloat16),
-            pltpu.VMEM(rows, jnp.bfloat16),
+            pltpu.SemaphoreType.REGULAR,
             sem((3,)),
         ]
-        + [sem((CHUNKS,))] * 7,
+        + [sem((CHUNKS,))] * 6,
         compiler_params=pltpu.CompilerParams(
-            collective_id=0, has_side_effects=True, vmem_limit_bytes=48 * 1024 * 1024
+            collective_id=0, has_side_effects=True, vmem_limit_bytes=63 * 1024 * 1024
         ),
         name="two_cores",
     )(query_rows.reshape(rows), key_rows.reshape(rows), value_rows.reshape(rows))

time: 122 us -> 115 us (0.943)
  Pallas kernels: 117 us -> 112 us
  local copies, waits for them, and re-layouts: 4.65 us -> 2.3 us
    pallas_call x1, Pallas kernels: 117 us -> 112 us  [local(): pl.pallas_call(kernel, out_shape=jax.ShapeDtypeStruct(rows, jnp.bfloat16)...]
    unnamed x7 -> x1, local copies, waits for them, and re-layouts: 4.65 us -> 2.3 us
where the time goes in v1:
time: 115 us
  Pallas kernels  112 us (97%)
  local copies, waits for them, and re-layouts  2.3 us (2%)
    pallas_call x1, Pallas kernels, local(): pl.pallas_call(kernel, out_shape=jax.ShapeDtypeStruct(rows, jnp.bfloat16)...  112 us
    unnamed x1, local copies, waits for them, and re-layouts  2.3 us

profile of v1, /device:TPU:1, one launch (start us, length us, event | category | flops | bytes accessed | tf_op | source)
XLA Modules:
  0.0 114.5 jit_solution(16430345525068100170)
XLA Ops:
  0.0 112.2 %two_cores.1 = bf16[256,2048]{1,0:T(8,128)(2,1)} custom-call(bf16[256,2048]{1,0:T(8,128)(2,1)} %bitcast.5, bf16[256,2048]{1,0:T(8,128)(2,1)} %bitcast.6, bf16[256,2048]{1,0:T(8,128)(2,1)} %bitcast.7), custom_call_target="tpu_custom_call" | custom-call | tf_op jit(solution)/shard_map/two_cores/pallas_call | solution.py:202
  112.2 2.3 %copy.5 = bf16[1,256,2048]{2,1,0:T(8,128)(2,1)} copy(bf16[1,256,2048]{2,1,0:T(8,128)(2,1)} %bitcast.4) | data formatting | bytes 2097152

commit v2 on v1

--- a/solution.py
+++ b/solution.py
@@ -21,7 +21,8 @@
 LINE = 8
 FLAT = 8
 STRIDE = 37
-REST_STRIDE = 18
+GROUPS = ((1, 4), (3, 5), (2, 7, 6))
+LINES = ((4, 3, 5, 2, 6, 1, 7), (1, 7, 2, 6, 3, 5, 4), (3, 5, 1, 7, 4, 2, 6))
 FAR_FIRST = sorted(
     range(1, FRAMES),
     key=lambda r: -(min(r // 8, 8 - r // 8) + 4 * (r // 4 % 2) + 0.5 * min(r % 4, 4 - r % 4)),
@@ -53,18 +54,16 @@
         return {"dp": clip, "ctx": peer}
 
     x, y, z = lax.rem(me, 4), lax.rem(me // 4, 2), me // 8
+    turn_x, turn_z = 1 + 2 * lax.rem(clip, 2), 1 + 6 * lax.rem(clip, 2)
 
     def moved(flat, line):
-        new_x, new_y = lax.rem(x + lax.rem(flat, 4), 4), lax.rem(y + flat // 4, 2)
-        return (lax.rem(z + line, LINE) * 2 + new_y) * 4 + new_x
+        new_x = lax.rem(x + lax.rem(flat, 4) * turn_x, 4)
+        new_y = lax.rem(y + flat // 4, 2)
+        return (lax.rem(z + line * turn_z, LINE) * 2 + new_y) * 4 + new_x
 
     def every(i):
         r = lax.rem(i * STRIDE, FRAMES)
         return moved(lax.rem(r, FLAT), r // FLAT)
-
-    def rest(i):
-        r = lax.rem(i * REST_STRIDE, (FLAT - 1) * (LINE - 1))
-        return moved(r // (LINE - 1) + 1, lax.rem(r, LINE - 1) + 1)
 
     barrier = pltpu.get_barrier_semaphore()
     for i in range(1, LINE):
@@ -72,8 +71,9 @@
     for i in range(1, FLAT):
         pl.semaphore_signal(barrier, inc=1, device_id=at(moved(i, 0)), device_id_type=MESH)
     pl.semaphore_wait(barrier, LINE + FLAT - 2)
-    for i in range(1, FLAT):
-        pl.semaphore_signal(ready, inc=1, device_id=at(moved(i, 0)), device_id_type=MESH)
+    for i in reversed(range(1, FLAT)):
+        back_to_me = (FLAT + 4 - i if i > 4 else 4 - i if i < 4 else 4)
+        pl.semaphore_signal(ready.at[back_to_me], inc=1, device_id=at(moved(i, 0)), device_id_type=MESH)
 
     def block(chunk, peer):
         rows = pl.ds(pl.multiple_of((peer // SLOTS) * PLACES, PLACES), PLACES)
@@ -97,10 +97,15 @@
             send_qk(chunk, moved(i, 0))
             send_qk(chunk, moved(0, i))
 
-    def send_qk_rest(chunk):
-        @pl.loop(0, (FLAT - 1) * (LINE - 1))
-        def _(i):
-            send_qk(chunk, rest(i))
+    def send_qk_lines(flats):
+        for flat in flats:
+            pl.semaphore_wait(ready.at[flat], 1)
+
+        @pl.loop(0, CHUNKS)
+        def _(chunk):
+            for i in range(LINE - 1):
+                for flat, lines in zip(flats, LINES):
+                    send_qk(chunk, moved(flat, lines[i]))
 
     def send_mid(chunk):
         rows, cols = block(chunk, me)
@@ -116,17 +121,22 @@
                 device_id=at(peer), device_id_type=MESH,
             ).start()
 
-    def send_back(chunk):
+    def keep_back(chunk):
         rows, cols = block(chunk, me)
         pltpu.make_async_copy(o_part.at[chunk, me], o_hbm.at[rows, cols], g_o.at[chunk]).start()
 
+    def send_back(chunk, low, high):
+        rows, cols = block(chunk, me)
         for r in FAR_FIRST:
             peer = moved(r % FLAT, r // FLAT)
-            pltpu.make_async_remote_copy(
-                src_ref=o_part.at[chunk, peer], dst_ref=o_hbm.at[rows, cols],
-                send_sem=s_o.at[chunk], recv_sem=g_o.at[chunk],
-                device_id=at(peer), device_id_type=MESH,
-            ).start()
+
+            @pl.when(jnp.logical_and(peer >= low * FLAT, peer < high * FLAT))
+            def _():
+                pltpu.make_async_remote_copy(
+                    src_ref=o_part.at[chunk, peer], dst_ref=o_hbm.at[rows, cols],
+                    send_sem=s_o.at[chunk], recv_sem=g_o.at[chunk],
+                    device_id=at(peer), device_id_type=MESH,
+                ).start()
 
     def arrived(ref, sem):
         pltpu.make_async_copy(ref, ref, sem).wait()
@@ -164,11 +174,8 @@
     def _(chunk):
         send_qk_near(chunk)
 
-    pl.semaphore_wait(ready, FLAT - 1)
-
-    @pl.loop(0, CHUNKS)
-    def _(chunk):
-        send_qk_rest(chunk)
+    for flats in GROUPS:
+        send_qk_lines(flats)
 
     loads[2].wait()
 
@@ -182,7 +189,18 @@
         arrived(r_qk.at[chunk], g_qk.at[chunk])
         arrived(r_v.at[chunk], g_v.at[chunk])
         temporal(chunk)
-        send_back(chunk)
+        keep_back(chunk)
+
+        @pl.when(chunk < CHUNKS - 2)
+        def _():
+            send_back(chunk, 0, LINE)
+
+        @pl.when(chunk >= CHUNKS - 2)
+        def _():
+            send_back(chunk, 0, 2)
+
+    for chunk in (CHUNKS - 2, CHUNKS - 1):
+        send_back(chunk, 2, LINE)
 
     for chunk in range(CHUNKS):
         cols = pl.ds(chunk * SLOTS * HD, SLOTS * HD)
@@ -213,7 +231,7 @@
             pltpu.VMEM((3, FRAMES * PLACES, HD), jnp.float32),
             pltpu.VMEM((FRAMES * PLACES, HD), jnp.float32),
             pltpu.VMEM((CHUNKS, FRAMES, PLACES, HD), jnp.bfloat16),
-            pltpu.SemaphoreType.REGULAR,
+            pltpu.SemaphoreType.REGULAR((FLAT,)),
             sem((3,)),
         ]
         + [sem((CHUNKS,))] * 6,

time: 115 us -> 113 us (0.983); the launches traced: 115 us -> 111 us
  Pallas kernels: 112 us -> 109 us
    pallas_call x1, Pallas kernels: 112 us -> 109 us  [local(): pl.pallas_call(kernel, out_shape=jax.ShapeDtypeStruct(rows, jnp.bfloat16)...]
where the time goes in v2:
time: 113 us; the launch traced here: 111 us
  Pallas kernels  109 us (96%)
  local copies, waits for them, and re-layouts  2.3 us (2%)
    pallas_call x1, Pallas kernels, local(): pl.pallas_call(kernel, out_shape=jax.ShapeDtypeStruct(rows, jnp.bfloat16)...  109 us
    unnamed x1, local copies, waits for them, and re-layouts  2.3 us

profile of v2, /device:TPU:1, one launch (start us, length us, event | category | flops | bytes accessed | tf_op | source)
XLA Modules:
  0.0 111.1 jit_solution(17438827678312161210)
XLA Ops:
  0.0 108.8 %two_cores.1 = bf16[256,2048]{1,0:T(8,128)(2,1)} custom-call(bf16[256,2048]{1,0:T(8,128)(2,1)} %bitcast.5, bf16[256,2048]{1,0:T(8,128)(2,1)} %bitcast.6, bf16[256,2048]{1,0:T(8,128)(2,1)} %bitcast.7), custom_call_target="tpu_custom_call" | custom-call | tf_op jit(solution)/shard_map/two_cores/pallas_call | solution.py:220
  108.8 2.3 %copy.5 = bf16[1,256,2048]{2,1,0:T(8,128)(2,1)} copy(bf16[1,256,2048]{2,1,0:T(8,128)(2,1)} %bitcast.4) | data formatting | bytes 2097152

commit v3 on v2

--- a/solution.py
+++ b/solution.py
@@ -40,7 +40,7 @@
     return jnp.dot(weights, v, preferred_element_type=jnp.float32)
 
 
-def kernel(q_hbm, k_hbm, v_hbm, o_hbm, qk, v, mid, r_qk, r_v, turned, back, o_part, ready, load, s_qk, s_v, s_o, g_qk, g_v, g_o):
+def kernel(q_hbm, k_hbm, v_hbm, o_ref, qk, v, mid, r_qk, r_v, turned, back, o_part, ready, load, s_qk, s_v, s_o, g_qk, g_v, g_o):
     clip, me = lax.axis_index("dp"), lax.axis_index("ctx")
     loads = [
         pltpu.make_async_copy(q_hbm, qk.at[0], load.at[0]),
@@ -123,7 +123,7 @@
 
     def keep_back(chunk):
         rows, cols = block(chunk, me)
-        pltpu.make_async_copy(o_part.at[chunk, me], o_hbm.at[rows, cols], g_o.at[chunk]).start()
+        pltpu.make_async_copy(o_part.at[chunk, me], o_ref.at[rows, cols], g_o.at[chunk]).start()
 
     def send_back(chunk, low, high):
         rows, cols = block(chunk, me)
@@ -133,7 +133,7 @@
             @pl.when(jnp.logical_and(peer >= low * FLAT, peer < high * FLAT))
             def _():
                 pltpu.make_async_remote_copy(
-                    src_ref=o_part.at[chunk, peer], dst_ref=o_hbm.at[rows, cols],
+                    src_ref=o_part.at[chunk, peer], dst_ref=o_ref.at[rows, cols],
                     send_sem=s_o.at[chunk], recv_sem=g_o.at[chunk],
                     device_id=at(peer), device_id_type=MESH,
                 ).start()
@@ -204,7 +204,7 @@
 
     for chunk in range(CHUNKS):
         cols = pl.ds(chunk * SLOTS * HD, SLOTS * HD)
-        arrived(o_hbm.at[:, cols], g_o.at[chunk])
+        arrived(o_ref.at[:, cols], g_o.at[chunk])
     for chunk in range(CHUNKS):
         sent = pl.ds(0, FRAMES - 1)
         arrived(r_qk.at[chunk, :, sent], s_qk.at[chunk])
@@ -219,9 +219,9 @@
     sem = pltpu.SemaphoreType.DMA
     result = pl.pallas_call(
         kernel,
-        out_shape=jax.ShapeDtypeStruct(rows, jnp.bfloat16),
+        out_shape=pltpu.VMEM(rows, jnp.bfloat16),
         in_specs=[anywhere] * 3,
-        out_specs=anywhere,
+        out_specs=pl.BlockSpec(memory_space=pltpu.VMEM),
         scratch_shapes=[
             pltpu.VMEM((2,) + rows, jnp.bfloat16),
             pltpu.VMEM(rows, jnp.bfloat16),
@@ -236,7 +236,7 @@
         ]
         + [sem((CHUNKS,))] * 6,
         compiler_params=pltpu.CompilerParams(
-            collective_id=0, has_side_effects=True, vmem_limit_bytes=63 * 1024 * 1024
+            collective_id=0, has_side_effects=True, vmem_limit_bytes=62 * 1024 * 1024
         ),
         name="two_cores",
     )(query_rows.reshape(rows), key_rows.reshape(rows), value_rows.reshape(rows))

time: 113 us -> 111 us (0.982)
  local copies, waits for them, and re-layouts: 2.3 us -> 0.97 us
    unnamed x1, local copies, waits for them, and re-layouts: 2.3 us -> 0.97 us
where the time goes in v3:
time: 111 us; the launch traced here: 110 us
  Pallas kernels  109 us (98%)
    pallas_call x1, Pallas kernels, local(): pl.pallas_call(kernel, out_shape=pltpu.VMEM(rows, jnp.bfloat16), in_specs...  109 us

profile of v3, /device:TPU:1, one launch (start us, length us, event | category | flops | bytes accessed | tf_op | source)
XLA Modules:
  0.0 110.0 jit_solution(1749586013766728912)
XLA Ops:
  0.0 109.0 %two_cores.1 = bf16[256,2048]{1,0:T(8,128)(2,1)S(1)} custom-call(bf16[256,2048]{1,0:T(8,128)(2,1)} %bitcast.5, bf16[256,2048]{1,0:T(8,128)(2,1)} %bitcast.6, bf16[256,2048]{1,0:T(8,128)(2,1)} %bitcast.7), custom_call_target="tpu_custom_call" | custom-call | tf_op jit(solution)/shard_map/two_cores/pallas_call | solution.py:220
  109.0 1.0 copy.5

commit v4 on v3

--- a/solution.py
+++ b/solution.py
@@ -29,18 +29,21 @@
 )
 
 
-def attend(q, k, v, keep=None):
+def weigh(q, k, keep=None):
     scores = lax.dot_general(q, k, (((1,), (1,)), ((), ())), preferred_element_type=jnp.float32)
     if keep is not None:
         scores = jnp.where(keep, scores, -jnp.inf)
     top = jnp.max(scores, axis=1, keepdims=True)
     weights = jnp.exp2((scores - top) * SCALE)
     total = jnp.sum(weights, axis=1, keepdims=True)
-    weights = (weights * (1.0 / total)).astype(jnp.bfloat16)
-    return jnp.dot(weights, v, preferred_element_type=jnp.float32)
-
-
-def kernel(q_hbm, k_hbm, v_hbm, o_ref, qk, v, mid, r_qk, r_v, turned, back, o_part, ready, load, s_qk, s_v, s_o, g_qk, g_v, g_o):
+    return (weights * (1.0 / total)).astype(jnp.bfloat16)
+
+
+def attend(q, k, v):
+    return jnp.dot(weigh(q, k), v, preferred_element_type=jnp.float32)
+
+
+def kernel(q_hbm, k_hbm, v_hbm, o_ref, qk, v, mid, r_qk, r_v, turned, shares, back, o_part, ready, load, s_qk, s_v, s_o, g_qk, g_v, g_o):
     clip, me = lax.axis_index("dp"), lax.axis_index("ctx")
     loads = [
         pltpu.make_async_copy(q_hbm, qk.at[0], load.at[0]),
@@ -151,18 +154,21 @@
     other = lax.broadcasted_iota(jnp.int32, (2 * FRAMES, 2 * FRAMES), 1) // FRAMES
     keep = side == other
 
-    def temporal(chunk):
+    def turn_two(a, t):
+        return jnp.concatenate(
+            [turned[a, pl.ds(t + s, FRAMES, stride=PLACES), :] for s in range(2)], axis=0
+        ).astype(jnp.bfloat16)
+
+    def temporal_weights(chunk):
         turned[0] = r_qk[chunk, 0].reshape(FRAMES * PLACES, HD).astype(jnp.float32)
         turned[1] = r_qk[chunk, 1].reshape(FRAMES * PLACES, HD).astype(jnp.float32)
+        for t in range(0, PLACES, 2):
+            shares[chunk, t // 2] = weigh(turn_two(0, t), turn_two(1, t), keep)
+
+    def temporal(chunk):
         turned[2] = r_v[chunk].reshape(FRAMES * PLACES, HD).astype(jnp.float32)
         for t in range(0, PLACES, 2):
-            trio = [
-                jnp.concatenate(
-                    [turned[a, pl.ds(t + s, FRAMES, stride=PLACES), :] for s in range(2)], axis=0
-                ).astype(jnp.bfloat16)
-                for a in range(3)
-            ]
-            both = attend(*trio, keep)
+            both = jnp.dot(shares[chunk, t // 2], turn_two(2, t), preferred_element_type=jnp.float32)
             back[pl.ds(t, FRAMES, stride=PLACES), :] = both[:FRAMES]
             back[pl.ds(t + 1, FRAMES, stride=PLACES), :] = both[FRAMES:]
         o_part[chunk] = back[...].astype(jnp.bfloat16).reshape(FRAMES, PLACES, HD)
@@ -187,6 +193,10 @@
     @pl.loop(0, CHUNKS)
     def _(chunk):
         arrived(r_qk.at[chunk], g_qk.at[chunk])
+        temporal_weights(chunk)
+
+    @pl.loop(0, CHUNKS)
+    def _(chunk):
         arrived(r_v.at[chunk], g_v.at[chunk])
         temporal(chunk)
         keep_back(chunk)
@@ -229,6 +239,7 @@
             pltpu.VMEM((CHUNKS, 2, FRAMES, PLACES, HD), jnp.bfloat16),
             pltpu.VMEM((CHUNKS, FRAMES, PLACES, HD), jnp.bfloat16),
             pltpu.VMEM((3, FRAMES * PLACES, HD), jnp.float32),
+            pltpu.VMEM((CHUNKS, PLACES // 2, 2 * FRAMES, 2 * FRAMES), jnp.bfloat16),
             pltpu.VMEM((FRAMES * PLACES, HD), jnp.float32),
             pltpu.VMEM((CHUNKS, FRAMES, PLACES, HD), jnp.bfloat16),
             pltpu.SemaphoreType.REGULAR((FLAT,)),

time: 111 us -> 111 us (level)
  no operation moved by 1% of the time
where the time goes in v4:
time: 111 us
  Pallas kernels  110 us (99%)
    pallas_call x1, Pallas kernels, local(): pl.pallas_call(kernel, out_shape=pltpu.VMEM(rows, jnp.bfloat16), in_specs...  110 us

profile of v4, /device:TPU:1, one launch (start us, length us, event | category | flops | bytes accessed | tf_op | source)
XLA Modules:
  0.0 110.8 jit_solution(14148332137762759720)
XLA Ops:
  0.0 109.9 %two_cores.1 = bf16[256,2048]{1,0:T(8,128)(2,1)S(1)} custom-call(bf16[256,2048]{1,0:T(8,128)(2,1)} %bitcast.5, bf16[256,2048]{1,0:T(8,128)(2,1)} %bitcast.6, bf16[256,2048]{1,0:T(8,128)(2,1)} %bitcast.7), custom_call_target="tpu_custom_call" | custom-call | tf_op jit(solution)/shard_map/two_cores/pallas_call | solution.py:230
  109.9 1.0 copy.5
